TPU v7x, 32 devices: a whole 2x2x4 slice. The times are simulated.
32 devices in a mesh: ctx: 8 (over z, y), head: 4 (over x, core).
Axes of the slice: x: 2, y: 2, z: 4, core: 2. Of those that a mesh axis runs over, the one named last changes fastest.
Arguments:
- queries: bfloat16 [8192, 512], P(('ctx', 'head')), may hold values from -27 to 27
- token_keys: bfloat16 [8192, 512], P(('ctx', 'head')), may hold values from -6 to 6
- token_values: bfloat16 [8192, 512], P(('ctx', 'head')), may hold values from -6 to 6
- grad_out: bfloat16 [8192, 512], P(('ctx', 'head')), may hold values from -48 to 48
- clip_gate: bfloat16 [16, 512], P(None, 'head'), may hold values from 0.099609375 to 1.8984375
- clip_lengths: int32 [16], replicated, may hold values from 1 to 1024, 8192 in all
Outputs:
- grad_queries: bfloat16 [8192, 512], P(('ctx', 'head'))
- grad_keys: bfloat16 [8192, 512], P(('ctx', 'head'))
- grad_values: bfloat16 [8192, 512], P(('ctx', 'head'))
- grad_gate: float32 [16, 512], P(None, 'head')
Inputs may be any that keep to these rules, and one draw needn't show every extreme that they name: `clip_lengths`: the clips fill the window in order; each attends only within itself.
All inputs are finite; a program needn't handle non-finite values.
Results may differ from a plain program's by a relative error of at most 0.03.
Values may be sent and summed in bfloat16 or wider, within the bound.
No kernel may reach another device: no remote copies, remote signals or barrier semaphores. Data moves between devices by JAX's collectives and lax.ppermute only.
A program may use at most 64 MiB of HBM per device.

v0:
```python
import functools
import math

import jax
import jax.numpy as jnp
from jax import lax
from jax.experimental import pallas as pl
from jax.experimental.pallas import tpu as pltpu
from jax.sharding import PartitionSpec as P

AXES = ("ctx", "head")
NEG = -1e30
NT = (((1,), (1,)), ((), ()))
NN = (((1,), (0,)), ((), ()))


def dot(left, right, dims):
    return lax.dot_general(left, right, dims, preferred_element_type=jnp.float32)


def toward(shift, blocks, heads):
    pairs = []
    for i in range(blocks):
        for j in range(heads):
            target = i + 1 if j >= heads // 2 else i - 1
            if 0 <= target < blocks:
                pairs.append((i * heads + j, target * heads + (j + shift) % heads))
    return pairs


def back(shift, blocks, heads):
    return [(b, a) for a, b in toward(shift, blocks, heads)]


def pack_kernel(heads, width, *refs):
    arrays, packed, sends = refs[:4], refs[4], refs[5 : 5 + heads]
    held, sem = refs[5 + heads :]
    me = lax.axis_index("head")
    copies = [pltpu.make_async_copy(array, held.at[n], sem.at[n]) for n, array in enumerate(arrays)]
    for copy in copies:
        copy.start()
    for n, copy in enumerate(copies):
        copy.wait()
        cols = slice(n * width, (n + 1) * width)
        for h in range(heads):
            packed[h, :, cols] = held[n, :, h * width : (h + 1) * width]
        for r in range(heads):
            head = lax.rem(me + r, heads)
            sends[r][:, cols] = held[n, :, pl.ds(pl.multiple_of(head * width, width), width)]


def pack(arrays, heads, width):
    part = arrays[0].shape[0]
    one = jax.ShapeDtypeStruct((part, 4 * width), jnp.bfloat16)
    vmem = pl.BlockSpec(memory_space=pltpu.VMEM)
    return pl.pallas_call(
        functools.partial(pack_kernel, heads, width),
        out_shape=[jax.ShapeDtypeStruct((heads, part, 4 * width), jnp.bfloat16)] + [one] * heads,
        in_specs=[pl.BlockSpec(memory_space=pltpu.HBM)] * 4,
        out_specs=[vmem] * (1 + heads),
        scratch_shapes=[pltpu.VMEM((4, part, heads * width), jnp.bfloat16), pltpu.SemaphoreType.DMA((4,))],
        compiler_params=pltpu.CompilerParams(vmem_limit_bytes=60 * 1024 * 1024),
    )(*arrays)


def attention_kernel(geometry, place, lengths, own, *refs):
    heads, rows, pad, width, scaling = geometry
    part = rows // heads
    halos, refs = refs[:heads], refs[heads:]
    gate, own_out = refs[:2]
    halo_outs, refs = refs[2 : 2 + heads], refs[2 + heads :]
    gate_out, span_out, win, result, keys_t, acc_k, acc_v, starts, sem = refs
    window = rows + 2 * pad
    per_exp = scaling * math.log2(math.e)
    block, me = place[0], place[1]
    clips = gate.shape[0]

    places = [(j, pad + rows + j * part if j < heads // 2 else (j - heads // 2) * part) for j in range(heads)]

    first = pltpu.make_async_copy(own, win.at[pl.ds(pad, rows), :], sem.at[0])
    first.start()
    for j, at_row in places:
        slot = lax.rem(me + heads - j, heads)
        for r in range(heads):

            @pl.when(slot == r)
            def _():
                pltpu.make_async_copy(halos[r], win.at[pl.ds(at_row, part), :], sem.at[1 + j]).start()

    def place_clip(c, carried):
        start, clip_low, clip_high, low, high = carried
        end = start + lengths[c]
        first_block, last_block = lax.div(start, rows), lax.div(end - 1, rows)
        edge = last_block * rows
        lower = (first_block != last_block) & (edge - start >= end - edge)
        owned = jnp.where(lower, first_block, last_block) == block
        starts[c] = start
        return (
            end,
            jnp.where(owned, jnp.minimum(clip_low, c), clip_low),
            jnp.where(owned, c + 1, clip_high),
            jnp.where(owned, jnp.minimum(low, start), low),
            jnp.where(owned, end, high),
        )

    most, zero = jnp.int32(2**30), jnp.int32(0)
    _, clip_low, clip_high, low, high = lax.fori_loop(0, clips, place_clip, (zero, most, zero, most, zero))
    span_out[0] = low
    span_out[1] = high
    gate_out[...] = jnp.zeros_like(gate_out)
    win[window:, :] = jnp.zeros((win.shape[0] - window, 4 * width), jnp.bfloat16)

    first.wait()
    for j, at_row in places:
        pltpu.make_async_copy(halos[0], win.at[pl.ds(at_row, part), :], sem.at[1 + j]).wait()

    def whole_clip(key_rows, query_rows, c, base, head, tail):
        at = pl.ds(base, key_rows)
        keys_t[:, :key_rows] = win[at, width : 2 * width].T
        acc_k[:key_rows, :] = jnp.zeros((key_rows, width), jnp.float32)
        acc_v[:key_rows, :] = jnp.zeros((key_rows, width), jnp.float32)
        row_gate = gate[pl.ds(c, 1), :]
        key_row = lax.broadcasted_iota(jnp.int32, (key_rows, query_rows), 0)

        def query_tile(j, _):
            q_at = pl.ds(pl.multiple_of(base + j * query_rows, 16), query_rows)
            query, grad = win[q_at, :width], win[q_at, 3 * width :]
            d_out = (row_gate * grad.astype(jnp.float32)).astype(jnp.bfloat16)
            s = dot(win[at, width : 2 * width], query, NT)
            s = jnp.where((key_row >= head) & (key_row < tail), s, NEG)
            top = jnp.max(s, axis=0, keepdims=True) * per_exp
            p = jnp.exp2(s * per_exp - top)
            dp = dot(win[at, 2 * width : 3 * width], d_out, NT)
            total = jnp.sum(p, axis=0, keepdims=True)
            weighted = jnp.sum(p * dp, axis=0, keepdims=True)
            column = j * query_rows + lax.broadcasted_iota(jnp.int32, (1, query_rows), 1)
            inverse = jnp.where((column >= head) & (column < tail), 1.0 / total, 0.0)
            p = p * inverse
            g = (p * (dp - weighted * inverse)).astype(jnp.bfloat16)
            acc_v[:key_rows, :] += dot(p.astype(jnp.bfloat16), grad, NN)
            acc_k[:key_rows, :] += dot(g, query, NN)
            new = (dot(keys_t[:, :key_rows], g, NN) * scaling).T
            row = j * query_rows + lax.broadcasted_iota(jnp.int32, (query_rows, width), 0)
            old = result[q_at, :width].astype(jnp.float32)
            result[q_at, :width] = jnp.where((row >= head) & (row < tail), new, old).astype(jnp.bfloat16)
            return 0

        lax.fori_loop(0, lax.div(tail + query_rows - 1, query_rows), query_tile, 0)
        values = acc_v[:key_rows, :]
        row = lax.broadcasted_iota(jnp.int32, (key_rows, width), 0)
        inside = (row >= head) & (row < tail)
        for n, new in ((1, acc_k[:key_rows, :] * scaling), (2, values * row_gate)):
            cols = slice(n * width, (n + 1) * width)
            old = result[at, cols].astype(jnp.float32)
            result[at, cols] = jnp.where(inside, new, old).astype(jnp.bfloat16)
        terms = values * win[at, 2 * width : 3 * width].astype(jnp.float32)
        gate_out[pl.ds(c, 1), :] = jnp.sum(terms, axis=0, keepdims=True)

    shapes = shapes_for(rows)
    origin = block * rows - pad

    def clip_step(c, _):
        start = starts[c] - origin
        base = pl.multiple_of(start // 16 * 16, 16)
        head = start - base
        tail = head + lengths[c]
        below = 0
        for key_rows, query_rows in shapes:

            @pl.when((tail > below) & (tail <= key_rows))
            def _():
                whole_clip(key_rows, query_rows, c, base, head, tail)

            below = key_rows
        return 0

    lax.fori_loop(clip_low, clip_high, clip_step, 0)

    last = pltpu.make_async_copy(result.at[pl.ds(pad, rows), :], own_out, sem.at[0])
    last.start()
    for j, at_row in places:
        slot = lax.rem(me + heads - j, heads)
        for r in range(heads):

            @pl.when(slot == r)
            def _():
                pltpu.make_async_copy(result.at[pl.ds(at_row, part), :], halo_outs[r], sem.at[1 + j]).start()
    last.wait()
    for j, at_row in places:
        pltpu.make_async_copy(result.at[pl.ds(at_row, part), :], halo_outs[0], sem.at[1 + j]).wait()


def shapes_for(rows):
    tile = rows // 4
    return [(n * tile, tile) for n in range(1, 5)] + [(rows + rows // 8, rows // 4 + rows // 8)]


def attention(place, lengths, own, halos, gate, heads, pad, width):
    rows = own.shape[0]
    part = rows // heads
    window = rows + 2 * pad
    spare = rows // 4
    anywhere = pl.BlockSpec(memory_space=pl.ANY)
    vmem = pl.BlockSpec(memory_space=pltpu.VMEM)
    smem = pl.BlockSpec(memory_space=pltpu.SMEM)
    geometry = (heads, rows, pad, width, width ** (-0.5))
    f32, b16 = jnp.float32, jnp.bfloat16
    most = shapes_for(rows)[-1][0]
    return pl.pallas_call(
        functools.partial(attention_kernel, geometry),
        out_shape=[jax.ShapeDtypeStruct((rows, 3 * width), b16)]
        + [jax.ShapeDtypeStruct((part, 3 * width), b16)] * heads
        + [jax.ShapeDtypeStruct(gate.shape, f32), jax.ShapeDtypeStruct((2,), jnp.int32)],
        in_specs=[smem] * 2 + [anywhere] * (1 + heads) + [vmem],
        out_specs=[anywhere] * (1 + heads) + [vmem, smem],
        scratch_shapes=[
            pltpu.VMEM((window + spare, 4 * width), b16),
            pltpu.VMEM((window + spare, 3 * width), b16),
            pltpu.VMEM((width, most), b16),
            pltpu.VMEM((most, width), f32),
            pltpu.VMEM((most, width), f32),
            pltpu.SMEM((gate.shape[0],), jnp.int32),
            pltpu.SemaphoreType.DMA((1 + heads,)),
        ],
        compiler_params=pltpu.CompilerParams(vmem_limit_bytes=48 * 1024 * 1024),
        cost_estimate=pl.CostEstimate(flops=4_000_000_000, bytes_accessed=4_000_000, transcendentals=4_000_000),
    )(place, lengths, own, *halos, gate)


def choose_kernel(heads, width, first_row, span, own, *refs):
    halos, outs = refs[:heads], refs[heads:]
    me = lax.axis_index("head")
    row = first_row[0] + lax.broadcasted_iota(jnp.int32, (own.shape[1], width), 0)
    keep = (row >= span[0]) & (row < span[1])
    for r in range(heads):
        head = lax.rem(me + r, heads)
        at = pl.ds(pl.multiple_of(head * width, width), width)
        kept, other = own[head].astype(jnp.float32), halos[r][...].astype(jnp.float32)
        for n, out in enumerate(outs):
            cols = slice(n * width, (n + 1) * width)
            out[:, at] = jnp.where(keep, kept[:, cols], other[:, cols]).astype(jnp.bfloat16)


def choose(first_row, span, own, halos, heads, width):
    part = own.shape[1]
    smem = pl.BlockSpec(memory_space=pltpu.SMEM)
    vmem = pl.BlockSpec(memory_space=pltpu.VMEM)
    return pl.pallas_call(
        functools.partial(choose_kernel, heads, width),
        out_shape=[jax.ShapeDtypeStruct((part, heads * width), jnp.bfloat16)] * 3,
        in_specs=[smem] * 2 + [vmem] * (1 + heads),
        out_specs=[vmem] * 3,
        compiler_params=pltpu.CompilerParams(vmem_limit_bytes=32 * 1024 * 1024),
    )(first_row, span, own, *halos)


def shards(heads, queries, token_keys, token_values, grad_out, clip_gate, clip_lengths):
    part, total_width = queries.shape
    width = total_width // heads
    rows = part * heads
    pad = rows // 2
    blocks = lax.axis_size("ctx")
    block, me = lax.axis_index("ctx"), lax.axis_index("head")

    packed, *sends = pack((queries, token_keys, token_values, grad_out), heads, width)
    own = lax.all_to_all(packed, "head", 0, 0, tiled=True).reshape(rows, 4 * width)
    halos = [lax.ppermute(sends[r], AXES, toward(r, blocks, heads)) for r in range(heads)]

    place = jnp.stack([block, me]).astype(jnp.int32)
    own_out, *rest = attention(
        place, clip_lengths, own, halos, clip_gate.astype(jnp.float32), heads, pad, width
    )
    halo_outs, gate_term, span = rest[:heads], rest[heads], rest[heads + 1]

    homes = [lax.ppermute(halo_outs[r], AXES, back(r, blocks, heads)) for r in range(heads)]
    mixed = lax.all_to_all(own_out.reshape(heads, part, 3 * width), "head", 0, 0, tiled=True)

    step = 1
    while step < blocks:
        gate_term = gate_term + lax.ppermute(gate_term, "ctx", [(i, i ^ step) for i in range(blocks)])
        step *= 2

    at = jnp.stack([rows * block + part * me]).astype(jnp.int32)
    grad_queries, grad_keys, grad_values = choose(at, span, mixed, homes, heads, width)
    return grad_queries, grad_keys, grad_values, gate_term


def solution(mesh):
    rows, columns = P(AXES, None), P(None, "head")
    return jax.shard_map(
        functools.partial(shards, mesh.shape["head"]),
        mesh=mesh,
        in_specs=(rows, rows, rows, rows, columns, P()),
        out_specs=(rows, rows, rows, columns),
        check_vma=False,
    )
```

profile of v0, /device:TPU:0, one launch (start us, length us, event | category | flops | bytes accessed | tf_op | source)
XLA Modules:
  0.0 84.3 jit_solution(17990398550146898164)
XLA Ops:
  0.6 2.7 %shard_map.93 = (bf16[4,256,512]{2,1,0:T(8,128)(2,1)}, bf16[256,512]{1,0:T(8,128)(2,1)}, bf16[256,512]{1,0:T(8,128)(2,1)}, bf16[256,512]{1,0:T(8,128)(2,1)}, bf16[256,512]{1,0:T(8,128)(2,1)}) custom-call(bf16[256,512]{1,0:T(8,128)(2,1)} %refs_0_.1, bf16[256,512]{1,0:T(8,128)(2,1)} %refs_1_.1, bf16[256,512]{1,0:T(8,128)(2,1)} %refs_2_.1, bf16[256,512]{1,0:T(8,128)(2,1)} %refs_3_.1), custom_call_target="tpu_custom_call" | custom-call | tf_op jit(solution)/shard_map/pallas_call | solution.py:56
  3.3 0.0 copy-start.4
  3.3 0.0 copy-start.3
  3.3 4.4 %all-to-all-start = ((bf16[4,256,512]{2,1,0:T(8,128)(2,1)}), bf16[4,256,512]{2,1,0:T(8,128)(2,1)S(1)}, u32[]{:S(2)}, u32[]{:S(2)}) async-start(bf16[4,256,512]{2,1,0:T(8,128)(2,1)} %get-tuple-element.19), calls=%async_computation | async-start | bytes 2097152 | tf_op jit(solution)/shard_map/all_to_all | solution.py:266
  7.7 1.3 %collective-permute-start = (bf16[256,512]{1,0:T(8,128)(2,1)}, bf16[256,512]{1,0:T(8,128)(2,1)S(1)}, u32[]{:S(2)}, u32[]{:S(2)}) collective-permute-start(bf16[256,512]{1,0:T(8,128)(2,1)} %get-tuple-element.20), channel_id=1, source_target_pairs={{2,6},{3,7},{4,0},{5,1},{6,10},{7,11},{8,4},{9,5},{10,14},{11,15},... | collective-permute-start | bytes 786440 | tf_op jit(solution)/shard_map/ppermute | solution.py:267
  9.0 0.7 collective-permute-start.1
  9.7 0.7 collective-permute-start.2
  10.4 1.3 %collective-permute-start.3 = (bf16[256,512]{1,0:T(8,128)(2,1)S(1)}, bf16[256,512]{1,0:T(8,128)(2,1)S(1)}, u32[]{:S(2)}, u32[]{:S(2)}) collective-permute-start(bf16[256,512]{1,0:T(8,128)(2,1)S(1)} %copy-done.2), channel_id=1, source_target_pairs={{2,5},{3,6},{4,3},{5,0},{6,9},{7,10},{8,7},{9,4},{10,13},{11,14},{... | collective-permute-start | bytes 786440 | tf_op jit(solution)/shard_map/ppermute | solution.py:267
  11.7 0.0 copy-start.1
  11.7 0.7 copy-done.1
  12.4 0.1 pad_add_fusion.place
  12.4 6.6 %collective-permute-done.refs_0_ = bf16[256,512]{1,0:T(8,128)(2,1)S(1)} collective-permute-done((bf16[256,512]{1,0:T(8,128)(2,1)}, bf16[256,512]{1,0:T(8,128)(2,1)S(1)}, u32[]{:S(2)}, u32[]{:S(2)}) %collective-permute-start) | collective-permute-done | bytes 262176 | tf_op jit(solution)/shard_map/ppermute | solution.py:267
  19.0 0.0 collective-permute-done.1.refs_1_
  19.0 0.0 collective-permute-done.2.refs_2_
  19.0 5.9 %collective-permute-done.3.refs_3_ = bf16[256,512]{1,0:T(8,128)(2,1)S(1)} collective-permute-done((bf16[256,512]{1,0:T(8,128)(2,1)S(1)}, bf16[256,512]{1,0:T(8,128)(2,1)S(1)}, u32[]{:S(2)}, u32[]{:S(2)}) %collective-permute-start.3) | collective-permute-done | bytes 262176 | tf_op jit(solution)/shard_map/ppermute | solution.py:267
  24.9 0.0 all-to-all-done
  24.9 7.4 %shard_map.94 = (bf16[1024,384]{1,0:T(8,128)(2,1)}, bf16[256,384]{1,0:T(8,128)(2,1)S(1)}, bf16[256,384]{1,0:T(8,128)(2,1)S(1)}, bf16[256,384]{1,0:T(8,128)(2,1)S...) custom-call(s32[2]{0:T(128)S(1)} %pad_add_fusion.place, s32[16]{0:T(128)S(1)} %copy-done, ...), custom_call_target="tpu_custom_call" | custom-call | flops 4000000000 | bytes 4000000 | tf_op jit(solution)/shard_map/pallas_call | solution.py:209
  32.3 13.2 %all-to-all-start.1 = ((bf16[4,256,384]{2,1,0:T(8,128)(2,1)}), bf16[4,256,384]{2,1,0:T(8,128)(2,1)S(1)}, u32[]{:S(2)}, u32[]{:S(2)}) async-start(bf16[4,256,384]{2,1,0:T(8,128)(2,1)} %bitcast.4), calls=%async_computation.1 | async-start | bytes 1572864 | tf_op jit(solution)/shard_map/all_to_all | solution.py:276
  45.5 8.6 %collective-permute-start.4 = (bf16[256,384]{1,0:T(8,128)(2,1)S(1)}, bf16[256,384]{1,0:T(8,128)(2,1)S(1)}, u32[]{:S(2)}, u32[]{:S(2)}) collective-permute-start(bf16[256,384]{1,0:T(8,128)(2,1)S(1)} %get-tuple-element.26), channel_id=1, source_target_pairs={{6,2},{7,3},{0,4},{1,5},{10,6},{11,7},{4,8},{5,9},{14,10},{15,11},... | collective-permute-start | bytes 589832 | tf_op jit(solution)/shard_map/ppermute | solution.py:275
  54.1 0.7 collective-permute-start.5
  54.8 0.7 collective-permute-start.6
  55.5 8.7 %collective-permute-start.7 = (bf16[256,384]{1,0:T(8,128)(2,1)S(1)}, bf16[256,384]{1,0:T(8,128)(2,1)S(1)}, u32[]{:S(2)}, u32[]{:S(2)}) collective-permute-start(bf16[256,384]{1,0:T(8,128)(2,1)S(1)} %get-tuple-element.29), channel_id=1, source_target_pairs={{5,2},{6,3},{3,4},{0,5},{9,6},{10,7},{7,8},{4,9},{13,10},{14,11},{... | collective-permute-start | bytes 589832 | tf_op jit(solution)/shard_map/ppermute | solution.py:275
  64.2 0.3 collective-permute-start.8
  64.5 7.1 %collective-permute-done.8 = f32[16,128]{1,0:T(8,128)S(1)} collective-permute-done((f32[16,128]{1,0:T(8,128)S(1)}, f32[16,128]{1,0:T(8,128)S(1)}, u32[]{:S(2)}, u32[]{:S(2)}) %collective-permute-start.8) | collective-permute-done | bytes 8224 | tf_op jit(solution)/shard_map/ppermute | solution.py:280
  71.7 4.2 %collective-permute-start.9 = (f32[16,128]{1,0:T(8,128)S(1)}, f32[16,128]{1,0:T(8,128)S(1)}, u32[]{:S(2)}, u32[]{:S(2)}) collective-permute-start(f32[16,128]{1,0:T(8,128)S(1)} %add.13), channel_id=1, source_target_pairs={{0,8},{4,12},{8,0},{12,4},{16,24},{20,28},{24,16},{28,20},{1,9},{5... | collective-permute-start | bytes 24584 | tf_op jit(solution)/shard_map/ppermute | solution.py:280
  75.9 1.6 %collective-permute-done.9 = f32[16,128]{1,0:T(8,128)S(1)} collective-permute-done((f32[16,128]{1,0:T(8,128)S(1)}, f32[16,128]{1,0:T(8,128)S(1)}, u32[]{:S(2)}, u32[]{:S(2)}) %collective-permute-start.9) | collective-permute-done | bytes 8224 | tf_op jit(solution)/shard_map/ppermute | solution.py:280
  77.5 2.8 %collective-permute-start.10 = (f32[16,128]{1,0:T(8,128)S(1)}, f32[16,128]{1,0:T(8,128)S(1)}, u32[]{:S(2)}, u32[]{:S(2)}) collective-permute-start(f32[16,128]{1,0:T(8,128)S(1)} %add.14), channel_id=1, source_target_pairs={{0,16},{4,20},{8,24},{12,28},{16,0},{20,4},{24,8},{28,12},{1,17},{... | collective-permute-start | bytes 24584 | tf_op jit(solution)/shard_map/ppermute | solution.py:280
  80.3 1.7 %collective-permute-done.10 = f32[16,128]{1,0:T(8,128)S(1)} collective-permute-done((f32[16,128]{1,0:T(8,128)S(1)}, f32[16,128]{1,0:T(8,128)S(1)}, u32[]{:S(2)}, u32[]{:S(2)}) %collective-permute-start.10) | collective-permute-done | bytes 8224 | tf_op jit(solution)/shard_map/ppermute | solution.py:280
  82.0 0.6 add.15
  82.7 0.0 collective-permute-done.4.refs_0_
  82.7 0.0 collective-permute-done.5.refs_1_
  82.7 1.6 %shard_map.95 = (bf16[256,512]{1,0:T(8,128)(2,1)}, bf16[256,512]{1,0:T(8,128)(2,1)}, bf16[256,512]{1,0:T(8,128)(2,1)}) custom-call(s32[1]{0:T(128)} %bitcast.first_row, s32[2]{0:T(128)S(1)} %get-tuple-element.24.span, bf16[4,256,384]{2,1,0:T(8,128)(2,1)S(1)} %all-to-all-done.1.own, bf16[256,384]{1,0:T(8,128)(2,1)S(1)} %collective-permute-done.4.refs_0_, ...), custom_call_target="tpu_custom_call" | custom-call | tf_op jit(solution)/shard_map/pallas_call | solution.py:248
  (12 shorter events, 0.0 us)
Async XLA Ops:
  3.3 5.7 %copy-start.4 = (bf16[256,512]{1,0:T(8,128)(2,1)S(1)}, bf16[256,512]{1,0:T(8,128)(2,1)}, u32[]{:S(2)}) copy-start(bf16[256,512]{1,0:T(8,128)(2,1)} %get-tuple-element.21) | copy-start | bytes 786436
  3.3 6.4 %copy-start.3 = (bf16[256,512]{1,0:T(8,128)(2,1)S(1)}, bf16[256,512]{1,0:T(8,128)(2,1)}, u32[]{:S(2)}) copy-start(bf16[256,512]{1,0:T(8,128)(2,1)} %get-tuple-element.22) | copy-start | bytes 786436
  3.3 7.0 %copy-start.2 = (bf16[256,512]{1,0:T(8,128)(2,1)S(1)}, bf16[256,512]{1,0:T(8,128)(2,1)}, u32[]{:S(2)}) copy-start(bf16[256,512]{1,0:T(8,128)(2,1)} %get-tuple-element.23) | copy-start | bytes 786436
  3.3 21.6 %all-to-all-start = ((bf16[4,256,512]{2,1,0:T(8,128)(2,1)}), bf16[4,256,512]{2,1,0:T(8,128)(2,1)S(1)}, u32[]{:S(2)}, u32[]{:S(2)}) async-start(bf16[4,256,512]{2,1,0:T(8,128)(2,1)} %get-tuple-element.19), calls=%async_computation | async-start | bytes 2097152 | tf_op jit(solution)/shard_map/all_to_all | solution.py:266
  7.7 11.3 %collective-permute-start = (bf16[256,512]{1,0:T(8,128)(2,1)}, bf16[256,512]{1,0:T(8,128)(2,1)S(1)}, u32[]{:S(2)}, u32[]{:S(2)}) collective-permute-start(bf16[256,512]{1,0:T(8,128)(2,1)} %get-tuple-element.20), channel_id=1, source_target_pairs={{2,6},{3,7},{4,0},{5,1},{6,10},{7,11},{8,4},{9,5},{10,14},{11,15},... | collective-permute-start | bytes 786440 | tf_op jit(solution)/shard_map/ppermute | solution.py:267
  9.0 10.0 %collective-permute-start.1 = (bf16[256,512]{1,0:T(8,128)(2,1)S(1)}, bf16[256,512]{1,0:T(8,128)(2,1)S(1)}, u32[]{:S(2)}, u32[]{:S(2)}) collective-permute-start(bf16[256,512]{1,0:T(8,128)(2,1)S(1)} %copy-done.4), channel_id=1, source_target_pairs={{2,7},{3,4},{4,1},{5,2},{6,11},{7,8},{8,5},{9,6},{10,15},{11,12},{... | collective-permute-start | bytes 786440 | tf_op jit(solution)/shard_map/ppermute | solution.py:267
  9.7 9.3 %collective-permute-start.2 = (bf16[256,512]{1,0:T(8,128)(2,1)S(1)}, bf16[256,512]{1,0:T(8,128)(2,1)S(1)}, u32[]{:S(2)}, u32[]{:S(2)}) collective-permute-start(bf16[256,512]{1,0:T(8,128)(2,1)S(1)} %copy-done.3), channel_id=1, source_target_pairs={{2,4},{3,5},{4,2},{5,3},{6,8},{7,9},{8,6},{9,7},{10,12},{11,13},{1... | collective-permute-start | bytes 786440 | tf_op jit(solution)/shard_map/ppermute | solution.py:267
  10.4 14.5 %collective-permute-start.3 = (bf16[256,512]{1,0:T(8,128)(2,1)S(1)}, bf16[256,512]{1,0:T(8,128)(2,1)S(1)}, u32[]{:S(2)}, u32[]{:S(2)}) collective-permute-start(bf16[256,512]{1,0:T(8,128)(2,1)S(1)} %copy-done.2), channel_id=1, source_target_pairs={{2,5},{3,6},{4,3},{5,0},{6,9},{7,10},{8,7},{9,4},{10,13},{11,14},{... | collective-permute-start | bytes 786440 | tf_op jit(solution)/shard_map/ppermute | solution.py:267
  11.7 0.7 copy-start.1
  12.4 12.4 %copy-start = (s32[16]{0:T(128)S(1)}, s32[16]{0:T(128)}, u32[]{:S(2)}) copy-start(s32[16]{0:T(128)} %lengths.1) | copy-start | bytes 196
  32.3 50.4 %all-to-all-start.1 = ((bf16[4,256,384]{2,1,0:T(8,128)(2,1)}), bf16[4,256,384]{2,1,0:T(8,128)(2,1)S(1)}, u32[]{:S(2)}, u32[]{:S(2)}) async-start(bf16[4,256,384]{2,1,0:T(8,128)(2,1)} %bitcast.4), calls=%async_computation.1 | async-start | bytes 1572864 | tf_op jit(solution)/shard_map/all_to_all | solution.py:276
  45.5 37.1 %collective-permute-start.4 = (bf16[256,384]{1,0:T(8,128)(2,1)S(1)}, bf16[256,384]{1,0:T(8,128)(2,1)S(1)}, u32[]{:S(2)}, u32[]{:S(2)}) collective-permute-start(bf16[256,384]{1,0:T(8,128)(2,1)S(1)} %get-tuple-element.26), channel_id=1, source_target_pairs={{6,2},{7,3},{0,4},{1,5},{10,6},{11,7},{4,8},{5,9},{14,10},{15,11},... | collective-permute-start | bytes 589832 | tf_op jit(solution)/shard_map/ppermute | solution.py:275
  54.1 28.6 %collective-permute-start.5 = (bf16[256,384]{1,0:T(8,128)(2,1)S(1)}, bf16[256,384]{1,0:T(8,128)(2,1)S(1)}, u32[]{:S(2)}, u32[]{:S(2)}) collective-permute-start(bf16[256,384]{1,0:T(8,128)(2,1)S(1)} %get-tuple-element.27), channel_id=1, source_target_pairs={{7,2},{4,3},{1,4},{2,5},{11,6},{8,7},{5,8},{6,9},{15,10},{12,11},{... | collective-permute-start | bytes 589832 | tf_op jit(solution)/shard_map/ppermute | solution.py:275
  54.8 27.9 %collective-permute-start.6 = (bf16[256,384]{1,0:T(8,128)(2,1)S(1)}, bf16[256,384]{1,0:T(8,128)(2,1)S(1)}, u32[]{:S(2)}, u32[]{:S(2)}) collective-permute-start(bf16[256,384]{1,0:T(8,128)(2,1)S(1)} %get-tuple-element.28), channel_id=1, source_target_pairs={{4,2},{5,3},{2,4},{3,5},{8,6},{9,7},{6,8},{7,9},{12,10},{13,11},{1... | collective-permute-start | bytes 589832 | tf_op jit(solution)/shard_map/ppermute | solution.py:275
  55.5 27.2 %collective-permute-start.7 = (bf16[256,384]{1,0:T(8,128)(2,1)S(1)}, bf16[256,384]{1,0:T(8,128)(2,1)S(1)}, u32[]{:S(2)}, u32[]{:S(2)}) collective-permute-start(bf16[256,384]{1,0:T(8,128)(2,1)S(1)} %get-tuple-element.29), channel_id=1, source_target_pairs={{5,2},{6,3},{3,4},{0,5},{9,6},{10,7},{7,8},{4,9},{13,10},{14,11},{... | collective-permute-start | bytes 589832 | tf_op jit(solution)/shard_map/ppermute | solution.py:275
  64.2 7.5 %collective-permute-start.8 = (f32[16,128]{1,0:T(8,128)S(1)}, f32[16,128]{1,0:T(8,128)S(1)}, u32[]{:S(2)}, u32[]{:S(2)}) collective-permute-start(f32[16,128]{1,0:T(8,128)S(1)} %get-tuple-element.33), channel_id=1, source_target_pairs={{0,4},{4,0},{8,12},{12,8},{16,20},{20,16},{24,28},{28,24},{1,5},{5... | collective-permute-start | bytes 24584 | tf_op jit(solution)/shard_map/ppermute | solution.py:280
  71.7 5.8 %collective-permute-start.9 = (f32[16,128]{1,0:T(8,128)S(1)}, f32[16,128]{1,0:T(8,128)S(1)}, u32[]{:S(2)}, u32[]{:S(2)}) collective-permute-start(f32[16,128]{1,0:T(8,128)S(1)} %add.13), channel_id=1, source_target_pairs={{0,8},{4,12},{8,0},{12,4},{16,24},{20,28},{24,16},{28,20},{1,9},{5... | collective-permute-start | bytes 24584 | tf_op jit(solution)/shard_map/ppermute | solution.py:280
  77.5 4.5 %collective-permute-start.10 = (f32[16,128]{1,0:T(8,128)S(1)}, f32[16,128]{1,0:T(8,128)S(1)}, u32[]{:S(2)}, u32[]{:S(2)}) collective-permute-start(f32[16,128]{1,0:T(8,128)S(1)} %add.14), channel_id=1, source_target_pairs={{0,16},{4,20},{8,24},{12,28},{16,0},{20,4},{24,8},{28,12},{1,17},{... | collective-permute-start | bytes 24584 | tf_op jit(solution)/shard_map/ppermute | solution.py:280
where the time goes:
time: 84.5 us; the launch traced here: 84.3 us
  starting transfers between devices  47.5 us (56%)
  waiting for transfers between devices  22.9 us (27%)
  Pallas kernels  11.7 us (14%)
    ppermute x4, starting transfers between devices, shards(): lax.ppermute(halo_outs[r], AXES, back(r, blocks, heads))  18.7 us
    all_to_all x1, starting transfers between devices, shards(): lax.all_to_all(own_out.reshape(heads, part, 3 * width), 'head', 0, 0, til...  13.2 us
    ppermute x4, waiting for transfers between devices, shards(): lax.ppermute(sends[r], AXES, toward(r, blocks, heads))  12.4 us
    ppermute x3, waiting for transfers between devices, shards(): lax.ppermute(gate_term, 'ctx', [(i, i ^ step) for i in range(blocks)])  10.5 us
    pallas_call x1, Pallas kernels, attention(): pl.pallas_call(functools.partial(attention_kernel, geometry), out_shape=[...  7.43 us
    ppermute x3, starting transfers between devices, shards(): lax.ppermute(gate_term, 'ctx', [(i, i ^ step) for i in range(blocks)])  7.32 us
    all_to_all x1, starting transfers between devices, shards(): lax.all_to_all(packed, 'head', 0, 0, tiled=True).reshape(rows, 4 * width)  4.35 us
    ppermute x4, starting transfers between devices, shards(): lax.ppermute(sends[r], AXES, toward(r, blocks, heads))  3.93 us
  transfers between devices with their start and end apart: 13, of which 5 were waited for; matrix products, arithmetic and copies ran while one was open for 1% of the time, Pallas kernels for 0%

commit v1 on v0

--- a/solution.py
+++ b/solution.py
@@ -9,6 +9,8 @@
 from jax.sharding import PartitionSpec as P
 
 AXES = ("ctx", "head")
+CHUNK = 256
+STRIP = 128
 NEG = -1e30
 NT = (((1,), (1,)), ((), ()))
 NN = (((1,), (0,)), ((), ()))
@@ -69,7 +71,7 @@
     halos, refs = refs[:heads], refs[heads:]
     gate, own_out = refs[:2]
     halo_outs, refs = refs[2 : 2 + heads], refs[2 + heads :]
-    gate_out, span_out, win, result, keys_t, acc_k, acc_v, starts, sem = refs
+    gate_out, span_out, win, result, keys_t, acc_k, acc_v, weight, dprob, starts, sem = refs
     window = rows + 2 * pad
     per_exp = scaling * math.log2(math.e)
     block, me = place[0], place[1]
@@ -114,30 +116,50 @@
     for j, at_row in places:
         pltpu.make_async_copy(halos[0], win.at[pl.ds(at_row, part), :], sem.at[1 + j]).wait()
 
-    def whole_clip(key_rows, query_rows, c, base, head, tail):
+    def whole_clip(key_rows, query_rows, below, c, base, head, tail):
         at = pl.ds(base, key_rows)
         keys_t[:, :key_rows] = win[at, width : 2 * width].T
         acc_k[:key_rows, :] = jnp.zeros((key_rows, width), jnp.float32)
         acc_v[:key_rows, :] = jnp.zeros((key_rows, width), jnp.float32)
         row_gate = gate[pl.ds(c, 1), :]
-        key_row = lax.broadcasted_iota(jnp.int32, (key_rows, query_rows), 0)
 
         def query_tile(j, _):
             q_at = pl.ds(pl.multiple_of(base + j * query_rows, 16), query_rows)
             query, grad = win[q_at, :width], win[q_at, 3 * width :]
             d_out = (row_gate * grad.astype(jnp.float32)).astype(jnp.bfloat16)
-            s = dot(win[at, width : 2 * width], query, NT)
-            s = jnp.where((key_row >= head) & (key_row < tail), s, NEG)
-            top = jnp.max(s, axis=0, keepdims=True) * per_exp
-            p = jnp.exp2(s * per_exp - top)
-            dp = dot(win[at, 2 * width : 3 * width], d_out, NT)
-            total = jnp.sum(p, axis=0, keepdims=True)
-            weighted = jnp.sum(p * dp, axis=0, keepdims=True)
+            tops, totals, dots = [], [], []
+            for k in range(0, key_rows, CHUNK):
+                rows_k = min(CHUNK, key_rows - k)
+                k_at = pl.ds(pl.multiple_of(base + k, 16), rows_k)
+                s_all = dot(win[k_at, width : 2 * width], query, NT)
+                dp_all = dot(win[k_at, 2 * width : 3 * width], d_out, NT)
+                for m in range(0, rows_k, STRIP):
+                    s, dp = s_all[m : m + STRIP], dp_all[m : m + STRIP]
+                    if k + m < 16 or k + m + STRIP > below:
+                        row = k + m + lax.broadcasted_iota(jnp.int32, s.shape, 0)
+                        s = jnp.where((row >= head) & (row < tail), s, NEG)
+                    top = jnp.max(s, axis=0, keepdims=True) * per_exp
+                    p = jnp.exp2(s * per_exp - top)
+                    weight[k + m : k + m + STRIP, :query_rows] = p
+                    dprob[k + m : k + m + STRIP, :query_rows] = dp
+                    tops.append(top)
+                    totals.append(jnp.sum(p, axis=0, keepdims=True))
+                    dots.append(jnp.sum(p * dp, axis=0, keepdims=True))
+            top = functools.reduce(jnp.maximum, tops)
+            scales = [jnp.exp2(t - top) for t in tops]
+            total = sum(t * f for t, f in zip(totals, scales))
+            weighted = sum(t * f for t, f in zip(dots, scales))
             column = j * query_rows + lax.broadcasted_iota(jnp.int32, (1, query_rows), 1)
             inverse = jnp.where((column >= head) & (column < tail), 1.0 / total, 0.0)
-            p = p * inverse
-            g = (p * (dp - weighted * inverse)).astype(jnp.bfloat16)
-            acc_v[:key_rows, :] += dot(p.astype(jnp.bfloat16), grad, NN)
+            row_dot = weighted * inverse
+            probs, grads = [], []
+            for n, f in enumerate(scales):
+                at_n = slice(n * STRIP, (n + 1) * STRIP)
+                p = weight[at_n, :query_rows] * (f * inverse)
+                probs.append(p.astype(jnp.bfloat16))
+                grads.append((p * (dprob[at_n, :query_rows] - row_dot)).astype(jnp.bfloat16))
+            g = jnp.concatenate(grads, axis=0)
+            acc_v[:key_rows, :] += dot(jnp.concatenate(probs, axis=0), grad, NN)
             acc_k[:key_rows, :] += dot(g, query, NN)
             new = (dot(keys_t[:, :key_rows], g, NN) * scaling).T
             row = j * query_rows + lax.broadcasted_iota(jnp.int32, (query_rows, width), 0)
@@ -168,8 +190,8 @@
         for key_rows, query_rows in shapes:
 
             @pl.when((tail > below) & (tail <= key_rows))
-            def _():
-                whole_clip(key_rows, query_rows, c, base, head, tail)
+            def _(below=below):
+                whole_clip(key_rows, query_rows, below, c, base, head, tail)
 
             below = key_rows
         return 0
@@ -205,7 +227,7 @@
     smem = pl.BlockSpec(memory_space=pltpu.SMEM)
     geometry = (heads, rows, pad, width, width ** (-0.5))
     f32, b16 = jnp.float32, jnp.bfloat16
-    most = shapes_for(rows)[-1][0]
+    most, widest = shapes_for(rows)[-1]
     return pl.pallas_call(
         functools.partial(attention_kernel, geometry),
         out_shape=[jax.ShapeDtypeStruct((rows, 3 * width), b16)]
@@ -219,6 +241,8 @@
             pltpu.VMEM((width, most), b16),
             pltpu.VMEM((most, width), f32),
             pltpu.VMEM((most, width), f32),
+            pltpu.VMEM((most, widest), f32),
+            pltpu.VMEM((most, widest), f32),
             pltpu.SMEM((gate.shape[0],), jnp.int32),
             pltpu.SemaphoreType.DMA((1 + heads,)),
         ],
@@ -272,13 +296,15 @@
     )
     halo_outs, gate_term, span = rest[:heads], rest[heads], rest[heads + 1]
 
-    homes = [lax.ppermute(halo_outs[r], AXES, back(r, blocks, heads)) for r in range(heads)]
-    mixed = lax.all_to_all(own_out.reshape(heads, part, 3 * width), "head", 0, 0, tiled=True)
-
-    step = 1
+    gate_term = gate_term + lax.ppermute(gate_term, "ctx", [(i, i ^ 1) for i in range(blocks)])
+    gate_term = gate_term + lax.ppermute(gate_term, "ctx", [(i, i ^ 2) for i in range(blocks)])
+    halo_outs[1], halo_outs[2], halo_outs[3], gate_term = lax.optimization_barrier((halo_outs[1], halo_outs[2], halo_outs[3], gate_term))
+    step = 4
     while step < blocks:
         gate_term = gate_term + lax.ppermute(gate_term, "ctx", [(i, i ^ step) for i in range(blocks)])
         step *= 2
+    mixed = lax.all_to_all(own_out.reshape(heads, part, 3 * width), "head", 0, 0, tiled=True)
+    homes = [lax.ppermute(halo_outs[r], AXES, back(r, blocks, heads)) for r in range(heads)]
 
     at = jnp.stack([rows * block + part * me]).astype(jnp.int32)
     grad_queries, grad_keys, grad_values = choose(at, span, mixed, homes, heads, width)

time: 84.5 us -> 80.4 us (0.951)
  the two profiles are of different devices: /device:TPU:0 before, /device:TPU:9 now
where the time goes in v1:
time: 80.4 us; the launch traced here: 79.8 us
  starting transfers between devices  40.8 us (51%)
  waiting for transfers between devices  24.3 us (30%)
  Pallas kernels  12.5 us (16%)
  between operations  0.82 us (1%)
    ppermute x4, starting transfers between devices, shards(): lax.ppermute(halo_outs[r], AXES, back(r, blocks, heads))  15.4 us
    ppermute x4, waiting for transfers between devices, shards(): lax.ppermute(sends[r], AXES, toward(r, blocks, heads))  14.8 us
    ppermute x4, starting transfers between devices, shards(): lax.ppermute(sends[r], AXES, toward(r, blocks, heads))  13.1 us
    pallas_call x1, Pallas kernels, attention(): pl.pallas_call(functools.partial(attention_kernel, geometry), out_shape=[...  8.24 us
    ppermute x1, waiting for transfers between devices, shards(): lax.ppermute(gate_term, 'ctx', [(i, i ^ step) for i in range(blocks)])  6.39 us
    ppermute x1, starting transfers between devices, shards(): lax.ppermute(gate_term, 'ctx', [(i, i ^ step) for i in range(blocks)])  4.41 us
    all_to_all x1, starting transfers between devices, shards(): lax.all_to_all(packed, 'head', 0, 0, tiled=True).reshape(rows, 4 * width)  4.3 us
    all_to_all x1, starting transfers between devices, shards(): lax.all_to_all(own_out.reshape(heads, part, 3 * width), 'head', 0, 0, til...  3.54 us
  transfers between devices with their start and end apart: 13, of which 6 were waited for; matrix products, arithmetic and copies ran while one was open for 1% of the time, Pallas kernels for 0%

profile of v1, /device:TPU:9, one launch (start us, length us, event | category | flops | bytes accessed | tf_op | source)
XLA Modules:
  0.0 79.8 jit_solution(16377896889400478641)
XLA Ops:
  0.6 2.6 %shard_map.93 = (bf16[4,256,512]{2,1,0:T(8,128)(2,1)}, bf16[256,512]{1,0:T(8,128)(2,1)}, bf16[256,512]{1,0:T(8,128)(2,1)}, bf16[256,512]{1,0:T(8,128)(2,1)}, bf16[256,512]{1,0:T(8,128)(2,1)}) custom-call(bf16[256,512]{1,0:T(8,128)(2,1)} %refs_0_.1, bf16[256,512]{1,0:T(8,128)(2,1)} %refs_1_.1, bf16[256,512]{1,0:T(8,128)(2,1)} %refs_2_.1, bf16[256,512]{1,0:T(8,128)(2,1)} %refs_3_.1), custom_call_target="tpu_custom_call" | custom-call | tf_op jit(solution)/shard_map/pallas_call | solution.py:58
  3.3 0.0 copy-start.5
  3.3 0.0 copy-start.4
  3.3 0.0 copy-start.3
  3.3 4.3 %all-to-all-start = ((bf16[4,256,512]{2,1,0:T(8,128)(2,1)}), bf16[4,256,512]{2,1,0:T(8,128)(2,1)S(1)}, u32[]{:S(2)}, u32[]{:S(2)}) async-start(bf16[4,256,512]{2,1,0:T(8,128)(2,1)} %get-tuple-element.23), calls=%async_computation | async-start | bytes 2097152 | tf_op jit(solution)/shard_map/all_to_all | solution.py:290
  7.6 3.0 %collective-permute-start = (bf16[256,512]{1,0:T(8,128)(2,1)S(1)}, bf16[256,512]{1,0:T(8,128)(2,1)S(1)}, u32[]{:S(2)}, u32[]{:S(2)}) collective-permute-start(bf16[256,512]{1,0:T(8,128)(2,1)S(1)} %copy-done.5), channel_id=1, source_target_pairs={{2,6},{3,7},{4,0},{5,1},{6,10},{7,11},{8,4},{9,5},{10,14},{11,15},... | collective-permute-start | bytes 786440 | tf_op jit(solution)/shard_map/ppermute | solution.py:291
  10.7 4.8 %collective-permute-start.1 = (bf16[256,512]{1,0:T(8,128)(2,1)S(1)}, bf16[256,512]{1,0:T(8,128)(2,1)S(1)}, u32[]{:S(2)}, u32[]{:S(2)}) collective-permute-start(bf16[256,512]{1,0:T(8,128)(2,1)S(1)} %copy-done.4), channel_id=1, source_target_pairs={{2,7},{3,4},{4,1},{5,2},{6,11},{7,8},{8,5},{9,6},{10,15},{11,12},{... | collective-permute-start | bytes 786440 | tf_op jit(solution)/shard_map/ppermute | solution.py:291
  15.5 2.5 %collective-permute-start.2 = (bf16[256,512]{1,0:T(8,128)(2,1)S(1)}, bf16[256,512]{1,0:T(8,128)(2,1)S(1)}, u32[]{:S(2)}, u32[]{:S(2)}) collective-permute-start(bf16[256,512]{1,0:T(8,128)(2,1)S(1)} %copy-done.3), channel_id=1, source_target_pairs={{2,4},{3,5},{4,2},{5,3},{6,8},{7,9},{8,6},{9,7},{10,12},{11,13},{1... | collective-permute-start | bytes 786440 | tf_op jit(solution)/shard_map/ppermute | solution.py:291
  18.0 2.8 %collective-permute-start.3 = (bf16[256,512]{1,0:T(8,128)(2,1)S(1)}, bf16[256,512]{1,0:T(8,128)(2,1)S(1)}, u32[]{:S(2)}, u32[]{:S(2)}) collective-permute-start(bf16[256,512]{1,0:T(8,128)(2,1)S(1)} %copy-done.2), channel_id=1, source_target_pairs={{2,5},{3,6},{4,3},{5,0},{6,9},{7,10},{8,7},{9,4},{10,13},{11,14},{... | collective-permute-start | bytes 786440 | tf_op jit(solution)/shard_map/ppermute | solution.py:291
  20.8 0.0 copy-start.1
  20.8 0.7 copy-done.1
  21.5 0.1 pad_add_fusion.place
  21.6 0.0 collective-permute-done.refs_0_
  21.6 0.7 collective-permute-done.1.refs_1_
  22.2 8.0 %collective-permute-done.2.refs_2_ = bf16[256,512]{1,0:T(8,128)(2,1)S(1)} collective-permute-done((bf16[256,512]{1,0:T(8,128)(2,1)S(1)}, bf16[256,512]{1,0:T(8,128)(2,1)S(1)}, u32[]{:S(2)}, u32[]{:S(2)}) %collective-permute-start.2) | collective-permute-done | bytes 262176 | tf_op jit(solution)/shard_map/ppermute | solution.py:291
  30.3 6.1 %collective-permute-done.3.refs_3_ = bf16[256,512]{1,0:T(8,128)(2,1)S(1)} collective-permute-done((bf16[256,512]{1,0:T(8,128)(2,1)S(1)}, bf16[256,512]{1,0:T(8,128)(2,1)S(1)}, u32[]{:S(2)}, u32[]{:S(2)}) %collective-permute-start.3) | collective-permute-done | bytes 262176 | tf_op jit(solution)/shard_map/ppermute | solution.py:291
  36.4 0.0 all-to-all-done
  36.4 8.2 %shard_map.94 = (bf16[1024,384]{1,0:T(8,128)(2,1)}, bf16[256,384]{1,0:T(8,128)(2,1)S(1)}, bf16[256,384]{1,0:T(8,128)(2,1)S(1)}, bf16[256,384]{1,0:T(8,128)(2,1)S...) custom-call(s32[2]{0:T(128)S(1)} %pad_add_fusion.place, s32[16]{0:T(128)S(1)} %copy-done, ...), custom_call_target="tpu_custom_call" | custom-call | flops 4000000000 | bytes 4000000 | tf_op jit(solution)/shard_map/pallas_call | solution.py:231
  44.7 3.5 %all-to-all-start.1 = ((bf16[4,256,384]{2,1,0:T(8,128)(2,1)}), bf16[4,256,384]{2,1,0:T(8,128)(2,1)S(1)}, u32[]{:S(2)}, u32[]{:S(2)}) async-start(bf16[4,256,384]{2,1,0:T(8,128)(2,1)} %bitcast.4), calls=%async_computation.1 | async-start | bytes 1572864 | tf_op jit(solution)/shard_map/all_to_all | solution.py:306
  48.2 0.0 collective-permute-start.5
  48.2 2.5 %collective-permute-done.5 = f32[16,128]{1,0:T(8,128)S(1)} collective-permute-done((f32[16,128]{1,0:T(8,128)S(1)}, f32[16,128]{1,0:T(8,128)S(1)}, u32[]{:S(2)}, u32[]{:S(2)}) %collective-permute-start.5) | collective-permute-done | bytes 8224 | tf_op jit(solution)/shard_map/ppermute | solution.py:299
  50.7 2.2 %collective-permute-start.4 = (bf16[256,384]{1,0:T(8,128)(2,1)S(1)}, bf16[256,384]{1,0:T(8,128)(2,1)S(1)}, u32[]{:S(2)}, u32[]{:S(2)}) collective-permute-start(bf16[256,384]{1,0:T(8,128)(2,1)S(1)} %get-tuple-element.30), channel_id=1, source_target_pairs={{6,2},{7,3},{0,4},{1,5},{10,6},{11,7},{4,8},{5,9},{14,10},{15,11},... | collective-permute-start | bytes 589832 | tf_op jit(solution)/shard_map/ppermute | solution.py:307
  52.9 0.6 collective-permute-done.6
  53.5 7.6 %collective-permute-start.7 = (bf16[256,384]{1,0:T(8,128)(2,1)S(1)}, bf16[256,384]{1,0:T(8,128)(2,1)S(1)}, u32[]{:S(2)}, u32[]{:S(2)}) collective-permute-start(bf16[256,384]{1,0:T(8,128)(2,1)S(1)} %get-tuple-element.35), channel_id=1, source_target_pairs={{7,2},{4,3},{1,4},{2,5},{11,6},{8,7},{5,8},{6,9},{15,10},{12,11},{... | collective-permute-start | bytes 589832 | tf_op jit(solution)/shard_map/ppermute | solution.py:307
  61.2 1.9 %collective-permute-start.8 = (bf16[256,384]{1,0:T(8,128)(2,1)S(1)}, bf16[256,384]{1,0:T(8,128)(2,1)S(1)}, u32[]{:S(2)}, u32[]{:S(2)}) collective-permute-start(bf16[256,384]{1,0:T(8,128)(2,1)S(1)} %get-tuple-element.36), channel_id=1, source_target_pairs={{4,2},{5,3},{2,4},{3,5},{8,6},{9,7},{6,8},{7,9},{12,10},{13,11},{1... | collective-permute-start | bytes 589832 | tf_op jit(solution)/shard_map/ppermute | solution.py:307
  63.1 3.7 %collective-permute-start.9 = (bf16[256,384]{1,0:T(8,128)(2,1)S(1)}, bf16[256,384]{1,0:T(8,128)(2,1)S(1)}, u32[]{:S(2)}, u32[]{:S(2)}) collective-permute-start(bf16[256,384]{1,0:T(8,128)(2,1)S(1)} %get-tuple-element.37), channel_id=1, source_target_pairs={{5,2},{6,3},{3,4},{0,5},{9,6},{10,7},{7,8},{4,9},{13,10},{14,11},{... | collective-permute-start | bytes 589832 | tf_op jit(solution)/shard_map/ppermute | solution.py:307
  66.8 4.4 %collective-permute-start.10 = (f32[16,128]{1,0:T(8,128)S(1)}, f32[16,128]{1,0:T(8,128)S(1)}, u32[]{:S(2)}, u32[]{:S(2)}) collective-permute-start(f32[16,128]{1,0:T(8,128)S(1)} %add.14), channel_id=1, source_target_pairs={{0,16},{4,20},{8,24},{12,28},{16,0},{20,4},{24,8},{28,12},{1,17},{... | collective-permute-start | bytes 24584 | tf_op jit(solution)/shard_map/ppermute | solution.py:304
  71.2 6.4 %collective-permute-done.10 = f32[16,128]{1,0:T(8,128)S(1)} collective-permute-done((f32[16,128]{1,0:T(8,128)S(1)}, f32[16,128]{1,0:T(8,128)S(1)}, u32[]{:S(2)}, u32[]{:S(2)}) %collective-permute-start.10) | collective-permute-done | bytes 8224 | tf_op jit(solution)/shard_map/ppermute | solution.py:304
  77.6 0.6 add.15
  78.2 0.0 collective-permute-done.8.refs_2_
  78.2 0.0 all-to-all-done.1.own
  78.2 1.6 %shard_map.95 = (bf16[256,512]{1,0:T(8,128)(2,1)}, bf16[256,512]{1,0:T(8,128)(2,1)}, bf16[256,512]{1,0:T(8,128)(2,1)}) custom-call(s32[1]{0:T(128)} %bitcast.first_row, s32[2]{0:T(128)S(1)} %get-tuple-element.28.span, bf16[4,256,384]{2,1,0:T(8,128)(2,1)S(1)} %all-to-all-done.1.own, bf16[256,384]{1,0:T(8,128)(2,1)S(1)} %collective-permute-done.4.refs_0_, ...), custom_call_target="tpu_custom_call" | custom-call | tf_op jit(solution)/shard_map/pallas_call | solution.py:272
  (14 shorter events, 0.0 us)
Async XLA Ops:
  3.3 4.3 %copy-start.5 = (bf16[256,512]{1,0:T(8,128)(2,1)S(1)}, bf16[256,512]{1,0:T(8,128)(2,1)}, u32[]{:S(2)}) copy-start(bf16[256,512]{1,0:T(8,128)(2,1)} %get-tuple-element.24) | copy-start | bytes 786436
  3.3 7.4 %copy-start.4 = (bf16[256,512]{1,0:T(8,128)(2,1)S(1)}, bf16[256,512]{1,0:T(8,128)(2,1)}, u32[]{:S(2)}) copy-start(bf16[256,512]{1,0:T(8,128)(2,1)} %get-tuple-element.25) | copy-start | bytes 786436
  3.3 12.2 %copy-start.3 = (bf16[256,512]{1,0:T(8,128)(2,1)S(1)}, bf16[256,512]{1,0:T(8,128)(2,1)}, u32[]{:S(2)}) copy-start(bf16[256,512]{1,0:T(8,128)(2,1)} %get-tuple-element.26) | copy-start | bytes 786436
  3.3 14.7 %copy-start.2 = (bf16[256,512]{1,0:T(8,128)(2,1)S(1)}, bf16[256,512]{1,0:T(8,128)(2,1)}, u32[]{:S(2)}) copy-start(bf16[256,512]{1,0:T(8,128)(2,1)} %get-tuple-element.27) | copy-start | bytes 786436
  3.3 33.1 %all-to-all-start = ((bf16[4,256,512]{2,1,0:T(8,128)(2,1)}), bf16[4,256,512]{2,1,0:T(8,128)(2,1)S(1)}, u32[]{:S(2)}, u32[]{:S(2)}) async-start(bf16[4,256,512]{2,1,0:T(8,128)(2,1)} %get-tuple-element.23), calls=%async_computation | async-start | bytes 2097152 | tf_op jit(solution)/shard_map/all_to_all | solution.py:290
  7.6 14.0 %collective-permute-start = (bf16[256,512]{1,0:T(8,128)(2,1)S(1)}, bf16[256,512]{1,0:T(8,128)(2,1)S(1)}, u32[]{:S(2)}, u32[]{:S(2)}) collective-permute-start(bf16[256,512]{1,0:T(8,128)(2,1)S(1)} %copy-done.5), channel_id=1, source_target_pairs={{2,6},{3,7},{4,0},{5,1},{6,10},{7,11},{8,4},{9,5},{10,14},{11,15},... | collective-permute-start | bytes 786440 | tf_op jit(solution)/shard_map/ppermute | solution.py:291
  10.7 11.6 %collective-permute-start.1 = (bf16[256,512]{1,0:T(8,128)(2,1)S(1)}, bf16[256,512]{1,0:T(8,128)(2,1)S(1)}, u32[]{:S(2)}, u32[]{:S(2)}) collective-permute-start(bf16[256,512]{1,0:T(8,128)(2,1)S(1)} %copy-done.4), channel_id=1, source_target_pairs={{2,7},{3,4},{4,1},{5,2},{6,11},{7,8},{8,5},{9,6},{10,15},{11,12},{... | collective-permute-start | bytes 786440 | tf_op jit(solution)/shard_map/ppermute | solution.py:291
  15.5 14.8 %collective-permute-start.2 = (bf16[256,512]{1,0:T(8,128)(2,1)S(1)}, bf16[256,512]{1,0:T(8,128)(2,1)S(1)}, u32[]{:S(2)}, u32[]{:S(2)}) collective-permute-start(bf16[256,512]{1,0:T(8,128)(2,1)S(1)} %copy-done.3), channel_id=1, source_target_pairs={{2,4},{3,5},{4,2},{5,3},{6,8},{7,9},{8,6},{9,7},{10,12},{11,13},{1... | collective-permute-start | bytes 786440 | tf_op jit(solution)/shard_map/ppermute | solution.py:291
  18.0 18.4 %collective-permute-start.3 = (bf16[256,512]{1,0:T(8,128)(2,1)S(1)}, bf16[256,512]{1,0:T(8,128)(2,1)S(1)}, u32[]{:S(2)}, u32[]{:S(2)}) collective-permute-start(bf16[256,512]{1,0:T(8,128)(2,1)S(1)} %copy-done.2), channel_id=1, source_target_pairs={{2,5},{3,6},{4,3},{5,0},{6,9},{7,10},{8,7},{9,4},{10,13},{11,14},{... | collective-permute-start | bytes 786440 | tf_op jit(solution)/shard_map/ppermute | solution.py:291
  20.8 0.7 copy-start.1
  21.6 14.8 %copy-start = (s32[16]{0:T(128)S(1)}, s32[16]{0:T(128)}, u32[]{:S(2)}) copy-start(s32[16]{0:T(128)} %lengths.1) | copy-start | bytes 196
  44.7 33.5 %all-to-all-start.1 = ((bf16[4,256,384]{2,1,0:T(8,128)(2,1)}), bf16[4,256,384]{2,1,0:T(8,128)(2,1)S(1)}, u32[]{:S(2)}, u32[]{:S(2)}) async-start(bf16[4,256,384]{2,1,0:T(8,128)(2,1)} %bitcast.4), calls=%async_computation.1 | async-start | bytes 1572864 | tf_op jit(solution)/shard_map/all_to_all | solution.py:306
  48.2 2.5 %collective-permute-start.5 = (f32[16,128]{1,0:T(8,128)S(1)}, f32[16,128]{1,0:T(8,128)S(1)}, u32[]{:S(2)}, u32[]{:S(2)}) collective-permute-start(f32[16,128]{1,0:T(8,128)S(1)} %get-tuple-element.34), channel_id=1, source_target_pairs={{0,4},{4,0},{8,12},{12,8},{16,20},{20,16},{24,28},{28,24},{1,5},{5... | collective-permute-start | bytes 24584 | tf_op jit(solution)/shard_map/ppermute | solution.py:299
  50.7 2.8 %collective-permute-start.6 = (f32[16,128]{1,0:T(8,128)S(1)}, f32[16,128]{1,0:T(8,128)S(1)}, u32[]{:S(2)}, u32[]{:S(2)}) collective-permute-start(f32[16,128]{1,0:T(8,128)S(1)} %add.13), channel_id=1, source_target_pairs={{0,8},{4,12},{8,0},{12,4},{16,24},{20,28},{24,16},{28,20},{1,9},{5... | collective-permute-start | bytes 24584 | tf_op jit(solution)/shard_map/ppermute | solution.py:300
  50.7 27.4 %collective-permute-start.4 = (bf16[256,384]{1,0:T(8,128)(2,1)S(1)}, bf16[256,384]{1,0:T(8,128)(2,1)S(1)}, u32[]{:S(2)}, u32[]{:S(2)}) collective-permute-start(bf16[256,384]{1,0:T(8,128)(2,1)S(1)} %get-tuple-element.30), channel_id=1, source_target_pairs={{6,2},{7,3},{0,4},{1,5},{10,6},{11,7},{4,8},{5,9},{14,10},{15,11},... | collective-permute-start | bytes 589832 | tf_op jit(solution)/shard_map/ppermute | solution.py:307
  53.5 24.6 %collective-permute-start.7 = (bf16[256,384]{1,0:T(8,128)(2,1)S(1)}, bf16[256,384]{1,0:T(8,128)(2,1)S(1)}, u32[]{:S(2)}, u32[]{:S(2)}) collective-permute-start(bf16[256,384]{1,0:T(8,128)(2,1)S(1)} %get-tuple-element.35), channel_id=1, source_target_pairs={{7,2},{4,3},{1,4},{2,5},{11,6},{8,7},{5,8},{6,9},{15,10},{12,11},{... | collective-permute-start | bytes 589832 | tf_op jit(solution)/shard_map/ppermute | solution.py:307
  61.2 17.0 %collective-permute-start.8 = (bf16[256,384]{1,0:T(8,128)(2,1)S(1)}, bf16[256,384]{1,0:T(8,128)(2,1)S(1)}, u32[]{:S(2)}, u32[]{:S(2)}) collective-permute-start(bf16[256,384]{1,0:T(8,128)(2,1)S(1)} %get-tuple-element.36), channel_id=1, source_target_pairs={{4,2},{5,3},{2,4},{3,5},{8,6},{9,7},{6,8},{7,9},{12,10},{13,11},{1... | collective-permute-start | bytes 589832 | tf_op jit(solution)/shard_map/ppermute | solution.py:307
  63.1 15.1 %collective-permute-start.9 = (bf16[256,384]{1,0:T(8,128)(2,1)S(1)}, bf16[256,384]{1,0:T(8,128)(2,1)S(1)}, u32[]{:S(2)}, u32[]{:S(2)}) collective-permute-start(bf16[256,384]{1,0:T(8,128)(2,1)S(1)} %get-tuple-element.37), channel_id=1, source_target_pairs={{5,2},{6,3},{3,4},{0,5},{9,6},{10,7},{7,8},{4,9},{13,10},{14,11},{... | collective-permute-start | bytes 589832 | tf_op jit(solution)/shard_map/ppermute | solution.py:307
  66.8 10.8 %collective-permute-start.10 = (f32[16,128]{1,0:T(8,128)S(1)}, f32[16,128]{1,0:T(8,128)S(1)}, u32[]{:S(2)}, u32[]{:S(2)}) collective-permute-start(f32[16,128]{1,0:T(8,128)S(1)} %add.14), channel_id=1, source_target_pairs={{0,16},{4,20},{8,24},{12,28},{16,0},{20,4},{24,8},{28,12},{1,17},{... | collective-permute-start | bytes 24584 | tf_op jit(solution)/shard_map/ppermute | solution.py:304

commit v2 on v1

--- a/solution.py
+++ b/solution.py
@@ -1,4 +1,5 @@
 import functools
+import itertools
 import math
 
 import jax
@@ -71,7 +72,7 @@
     halos, refs = refs[:heads], refs[heads:]
     gate, own_out = refs[:2]
     halo_outs, refs = refs[2 : 2 + heads], refs[2 + heads :]
-    gate_out, span_out, win, result, keys_t, acc_k, acc_v, weight, dprob, starts, sem = refs
+    gate_out, span_out, win, result, keys_t, acc_k, acc_v, *held, starts, sem = refs
     window = rows + 2 * pad
     per_exp = scaling * math.log2(math.e)
     block, me = place[0], place[1]
@@ -119,14 +120,13 @@
     def whole_clip(key_rows, query_rows, below, c, base, head, tail):
         at = pl.ds(base, key_rows)
         keys_t[:, :key_rows] = win[at, width : 2 * width].T
-        acc_k[:key_rows, :] = jnp.zeros((key_rows, width), jnp.float32)
-        acc_v[:key_rows, :] = jnp.zeros((key_rows, width), jnp.float32)
         row_gate = gate[pl.ds(c, 1), :]
 
-        def query_tile(j, _):
+        def scores(j):
             q_at = pl.ds(pl.multiple_of(base + j * query_rows, 16), query_rows)
             query, grad = win[q_at, :width], win[q_at, 3 * width :]
             d_out = (row_gate * grad.astype(jnp.float32)).astype(jnp.bfloat16)
+            weight, dprob = held[2 * (j % 2)], held[2 * (j % 2) + 1]
             tops, totals, dots = [], [], []
             for k in range(0, key_rows, CHUNK):
                 rows_k = min(CHUNK, key_rows - k)
@@ -145,29 +145,45 @@
                     tops.append(top)
                     totals.append(jnp.sum(p, axis=0, keepdims=True))
                     dots.append(jnp.sum(p * dp, axis=0, keepdims=True))
+                yield None
             top = functools.reduce(jnp.maximum, tops)
             scales = [jnp.exp2(t - top) for t in tops]
             total = sum(t * f for t, f in zip(totals, scales))
             weighted = sum(t * f for t, f in zip(dots, scales))
             column = j * query_rows + lax.broadcasted_iota(jnp.int32, (1, query_rows), 1)
             inverse = jnp.where((column >= head) & (column < tail), 1.0 / total, 0.0)
-            row_dot = weighted * inverse
-            probs, grads = [], []
-            for n, f in enumerate(scales):
-                at_n = slice(n * STRIP, (n + 1) * STRIP)
-                p = weight[at_n, :query_rows] * (f * inverse)
-                probs.append(p.astype(jnp.bfloat16))
-                grads.append((p * (dprob[at_n, :query_rows] - row_dot)).astype(jnp.bfloat16))
-            g = jnp.concatenate(grads, axis=0)
-            acc_v[:key_rows, :] += dot(jnp.concatenate(probs, axis=0), grad, NN)
-            acc_k[:key_rows, :] += dot(g, query, NN)
-            new = (dot(keys_t[:, :key_rows], g, NN) * scaling).T
+            yield j, q_at, [f * inverse for f in scales], weighted * inverse
+
+        def gradients(state):
+            j, q_at, scales, row_dot = state
+            query, grad = win[q_at, :width], win[q_at, 3 * width :]
+            weight, dprob = held[2 * (j % 2)], held[2 * (j % 2) + 1]
+            kept = []
+            for k in range(0, key_rows, CHUNK):
+                upto = min(k + CHUNK, key_rows)
+                probs, grads = [], []
+                for m in range(k, upto, STRIP):
+                    p = weight[m : m + STRIP, :query_rows] * scales[m // STRIP]
+                    probs.append(p.astype(jnp.bfloat16))
+                    grads.append((p * (dprob[m : m + STRIP, :query_rows] - row_dot)).astype(jnp.bfloat16))
+                p, g = jnp.concatenate(probs, axis=0), jnp.concatenate(grads, axis=0)
+                kept.append(g)
+                for acc, term in ((acc_v, dot(p, grad, NN)), (acc_k, dot(g, query, NN))):
+                    acc[k:upto, :] = term if j == 0 else acc[k:upto, :] + term
+                yield None
+            new = (dot(keys_t[:, :key_rows], jnp.concatenate(kept, axis=0), NN) * scaling).T
             row = j * query_rows + lax.broadcasted_iota(jnp.int32, (query_rows, width), 0)
             old = result[q_at, :width].astype(jnp.float32)
             result[q_at, :width] = jnp.where((row >= head) & (row < tail), new, old).astype(jnp.bfloat16)
-            return 0
-
-        lax.fori_loop(0, lax.div(tail + query_rows - 1, query_rows), query_tile, 0)
+            yield None
+
+        state = None
+        for j in range(-(-key_rows // query_rows) + 1):
+            ahead = scores(j) if j * query_rows < key_rows else iter(())
+            behind = gradients(state) if j > 0 else iter(())
+            for state, _ in itertools.zip_longest(ahead, behind):
+                pass
+
         values = acc_v[:key_rows, :]
         row = lax.broadcasted_iota(jnp.int32, (key_rows, width), 0)
         inside = (row >= head) & (row < tail)
@@ -241,8 +257,7 @@
             pltpu.VMEM((width, most), b16),
             pltpu.VMEM((most, width), f32),
             pltpu.VMEM((most, width), f32),
-            pltpu.VMEM((most, widest), f32),
-            pltpu.VMEM((most, widest), f32),
+            *[pltpu.VMEM((most, widest), f32)] * 4,
             pltpu.SMEM((gate.shape[0],), jnp.int32),
             pltpu.SemaphoreType.DMA((1 + heads,)),
         ],

time: 80.4 us -> 77.6 us (0.965)
  the two profiles are of different devices: /device:TPU:9 before, /device:TPU:1 now
where the time goes in v2:
time: 77.6 us; the launch traced here: 77.1 us
  starting transfers between devices  49.4 us (64%)
  waiting for transfers between devices  15.4 us (20%)
  Pallas kernels  10.1 us (13%)
  between operations  0.84 us (1%)
    all_to_all x1, starting transfers between devices, shards(): lax.all_to_all(own_out.reshape(heads, part, 3 * width), 'head', 0, 0, til...  16.9 us
    ppermute x4, waiting for transfers between devices, shards(): lax.ppermute(sends[r], AXES, toward(r, blocks, heads))  8.77 us
    ppermute x1, starting transfers between devices, shards(): lax.ppermute(gate_term, 'ctx', [(i, i ^ step) for i in range(blocks)])  8.12 us
    ppermute x4, starting transfers between devices, shards(): lax.ppermute(halo_outs[r], AXES, back(r, blocks, heads))  7.66 us
    pallas_call x1, Pallas kernels, attention(): pl.pallas_call(functools.partial(attention_kernel, geometry), out_shape=[...  5.8 us
    ppermute x1, waiting for transfers between devices, shards(): lax.ppermute(gate_term, 'ctx', [(i, i ^ step) for i in range(blocks)])  5.61 us
    ppermute x1, starting transfers between devices, shards(): lax.ppermute(gate_term, 'ctx', [(i, i ^ 1) for i in range(blocks)])  5.5 us
    all_to_all x1, starting transfers between devices, shards(): lax.all_to_all(packed, 'head', 0, 0, tiled=True).reshape(rows, 4 * width)  4.41 us
  transfers between devices with their start and end apart: 13, of which 4 were waited for; matrix products, arithmetic and copies ran while one was open for 1% of the time, Pallas kernels for 0%

profile of v2, /device:TPU:1, one launch (start us, length us, event | category | flops | bytes accessed | tf_op | source)
XLA Modules:
  0.0 77.1 jit_solution(2074394216913268174)
XLA Ops:
  0.6 2.6 %shard_map.93 = (bf16[4,256,512]{2,1,0:T(8,128)(2,1)}, bf16[256,512]{1,0:T(8,128)(2,1)}, bf16[256,512]{1,0:T(8,128)(2,1)}, bf16[256,512]{1,0:T(8,128)(2,1)}, bf16[256,512]{1,0:T(8,128)(2,1)}) custom-call(bf16[256,512]{1,0:T(8,128)(2,1)} %refs_0_.1, bf16[256,512]{1,0:T(8,128)(2,1)} %refs_1_.1, bf16[256,512]{1,0:T(8,128)(2,1)} %refs_2_.1, bf16[256,512]{1,0:T(8,128)(2,1)} %refs_3_.1), custom_call_target="tpu_custom_call" | custom-call | tf_op jit(solution)/shard_map/pallas_call | solution.py:59
  3.3 0.0 copy-start.5
  3.3 0.0 copy-start.4
  3.3 0.0 copy-start.3
  3.3 4.4 %all-to-all-start = ((bf16[4,256,512]{2,1,0:T(8,128)(2,1)}), bf16[4,256,512]{2,1,0:T(8,128)(2,1)S(1)}, u32[]{:S(2)}, u32[]{:S(2)}) async-start(bf16[4,256,512]{2,1,0:T(8,128)(2,1)} %get-tuple-element.23), calls=%async_computation | async-start | bytes 2097152 | tf_op jit(solution)/shard_map/all_to_all | solution.py:305
  7.7 1.3 %collective-permute-start = (bf16[256,512]{1,0:T(8,128)(2,1)S(1)}, bf16[256,512]{1,0:T(8,128)(2,1)S(1)}, u32[]{:S(2)}, u32[]{:S(2)}) collective-permute-start(bf16[256,512]{1,0:T(8,128)(2,1)S(1)} %copy-done.5), channel_id=1, source_target_pairs={{2,6},{3,7},{4,0},{5,1},{6,10},{7,11},{8,4},{9,5},{10,14},{11,15},... | collective-permute-start | bytes 786440 | tf_op jit(solution)/shard_map/ppermute | solution.py:306
  9.0 1.3 %collective-permute-start.1 = (bf16[256,512]{1,0:T(8,128)(2,1)S(1)}, bf16[256,512]{1,0:T(8,128)(2,1)S(1)}, u32[]{:S(2)}, u32[]{:S(2)}) collective-permute-start(bf16[256,512]{1,0:T(8,128)(2,1)S(1)} %copy-done.4), channel_id=1, source_target_pairs={{2,7},{3,4},{4,1},{5,2},{6,11},{7,8},{8,5},{9,6},{10,15},{11,12},{... | collective-permute-start | bytes 786440 | tf_op jit(solution)/shard_map/ppermute | solution.py:306
  10.4 0.7 collective-permute-start.2
  11.0 0.7 collective-permute-start.3
  11.7 0.0 copy-start.1
  11.7 0.7 copy-done.1
  12.4 0.1 pad_add_fusion.place
  12.5 5.7 %collective-permute-done.refs_0_ = bf16[256,512]{1,0:T(8,128)(2,1)S(1)} collective-permute-done((bf16[256,512]{1,0:T(8,128)(2,1)S(1)}, bf16[256,512]{1,0:T(8,128)(2,1)S(1)}, u32[]{:S(2)}, u32[]{:S(2)}) %collective-permute-start) | collective-permute-done | bytes 262176 | tf_op jit(solution)/shard_map/ppermute | solution.py:306
  18.2 3.0 %collective-permute-done.1.refs_1_ = bf16[256,512]{1,0:T(8,128)(2,1)S(1)} collective-permute-done((bf16[256,512]{1,0:T(8,128)(2,1)S(1)}, bf16[256,512]{1,0:T(8,128)(2,1)S(1)}, u32[]{:S(2)}, u32[]{:S(2)}) %collective-permute-start.1) | collective-permute-done | bytes 262176 | tf_op jit(solution)/shard_map/ppermute | solution.py:306
  21.3 0.0 collective-permute-done.3.refs_3_
  21.3 0.0 all-to-all-done
  21.3 5.8 %shard_map.94 = (bf16[1024,384]{1,0:T(8,128)(2,1)}, bf16[256,384]{1,0:T(8,128)(2,1)S(1)}, bf16[256,384]{1,0:T(8,128)(2,1)S(1)}, bf16[256,384]{1,0:T(8,128)(2,1)S...) custom-call(s32[2]{0:T(128)S(1)} %pad_add_fusion.place, s32[16]{0:T(128)S(1)} %copy-done, ...), custom_call_target="tpu_custom_call" | custom-call | flops 4000000000 | bytes 4000000 | tf_op jit(solution)/shard_map/pallas_call | solution.py:247
  27.1 16.9 %all-to-all-start.1 = ((bf16[4,256,384]{2,1,0:T(8,128)(2,1)}), bf16[4,256,384]{2,1,0:T(8,128)(2,1)S(1)}, u32[]{:S(2)}, u32[]{:S(2)}) async-start(bf16[4,256,384]{2,1,0:T(8,128)(2,1)} %bitcast.4), calls=%async_computation.1 | async-start | bytes 1572864 | tf_op jit(solution)/shard_map/all_to_all | solution.py:321
  44.0 5.5 %collective-permute-start.5 = (f32[16,128]{1,0:T(8,128)S(1)}, f32[16,128]{1,0:T(8,128)S(1)}, u32[]{:S(2)}, u32[]{:S(2)}) collective-permute-start(f32[16,128]{1,0:T(8,128)S(1)} %get-tuple-element.34), channel_id=1, source_target_pairs={{0,4},{4,0},{8,12},{12,8},{16,20},{20,16},{24,28},{28,24},{1,5},{5... | collective-permute-start | bytes 24584 | tf_op jit(solution)/shard_map/ppermute | solution.py:314
  49.5 1.0 %collective-permute-done.5 = f32[16,128]{1,0:T(8,128)S(1)} collective-permute-done((f32[16,128]{1,0:T(8,128)S(1)}, f32[16,128]{1,0:T(8,128)S(1)}, u32[]{:S(2)}, u32[]{:S(2)}) %collective-permute-start.5) | collective-permute-done | bytes 8224 | tf_op jit(solution)/shard_map/ppermute | solution.py:314
  50.5 2.9 %collective-permute-start.6 = (f32[16,128]{1,0:T(8,128)S(1)}, f32[16,128]{1,0:T(8,128)S(1)}, u32[]{:S(2)}, u32[]{:S(2)}) collective-permute-start(f32[16,128]{1,0:T(8,128)S(1)} %add.13), channel_id=1, source_target_pairs={{0,8},{4,12},{8,0},{12,4},{16,24},{20,28},{24,16},{28,20},{1,9},{5... | collective-permute-start | bytes 24584 | tf_op jit(solution)/shard_map/ppermute | solution.py:315
  53.4 2.2 %collective-permute-start.4 = (bf16[256,384]{1,0:T(8,128)(2,1)S(1)}, bf16[256,384]{1,0:T(8,128)(2,1)S(1)}, u32[]{:S(2)}, u32[]{:S(2)}) collective-permute-start(bf16[256,384]{1,0:T(8,128)(2,1)S(1)} %get-tuple-element.30), channel_id=1, source_target_pairs={{6,2},{7,3},{0,4},{1,5},{10,6},{11,7},{4,8},{5,9},{14,10},{15,11},... | collective-permute-start | bytes 589832 | tf_op jit(solution)/shard_map/ppermute | solution.py:322
  55.6 0.0 collective-permute-done.6
  55.6 4.1 %collective-permute-start.7 = (bf16[256,384]{1,0:T(8,128)(2,1)S(1)}, bf16[256,384]{1,0:T(8,128)(2,1)S(1)}, u32[]{:S(2)}, u32[]{:S(2)}) collective-permute-start(bf16[256,384]{1,0:T(8,128)(2,1)S(1)} %get-tuple-element.35), channel_id=1, source_target_pairs={{7,2},{4,3},{1,4},{2,5},{11,6},{8,7},{5,8},{6,9},{15,10},{12,11},{... | collective-permute-start | bytes 589832 | tf_op jit(solution)/shard_map/ppermute | solution.py:322
  59.7 0.7 collective-permute-start.8
  60.4 0.7 collective-permute-start.9
  61.1 8.1 %collective-permute-start.10 = (f32[16,128]{1,0:T(8,128)S(1)}, f32[16,128]{1,0:T(8,128)S(1)}, u32[]{:S(2)}, u32[]{:S(2)}) collective-permute-start(f32[16,128]{1,0:T(8,128)S(1)} %add.14), channel_id=1, source_target_pairs={{0,16},{4,20},{8,24},{12,28},{16,0},{20,4},{24,8},{28,12},{1,17},{... | collective-permute-start | bytes 24584 | tf_op jit(solution)/shard_map/ppermute | solution.py:319
  69.2 5.6 %collective-permute-done.10 = f32[16,128]{1,0:T(8,128)S(1)} collective-permute-done((f32[16,128]{1,0:T(8,128)S(1)}, f32[16,128]{1,0:T(8,128)S(1)}, u32[]{:S(2)}, u32[]{:S(2)}) %collective-permute-start.10) | collective-permute-done | bytes 8224 | tf_op jit(solution)/shard_map/ppermute | solution.py:319
  74.8 0.6 add.15
  75.4 0.0 collective-permute-done.7.refs_1_
  75.4 0.0 collective-permute-done.8.refs_2_
  75.5 1.6 %shard_map.95 = (bf16[256,512]{1,0:T(8,128)(2,1)}, bf16[256,512]{1,0:T(8,128)(2,1)}, bf16[256,512]{1,0:T(8,128)(2,1)}) custom-call(s32[1]{0:T(128)} %bitcast.first_row, s32[2]{0:T(128)S(1)} %get-tuple-element.28.span, bf16[4,256,384]{2,1,0:T(8,128)(2,1)S(1)} %all-to-all-done.1.own, bf16[256,384]{1,0:T(8,128)(2,1)S(1)} %collective-permute-done.4.refs_0_, ...), custom_call_target="tpu_custom_call" | custom-call | tf_op jit(solution)/shard_map/pallas_call | solution.py:287
  (14 shorter events, 0.0 us)
Async XLA Ops:
  3.3 4.5 %copy-start.5 = (bf16[256,512]{1,0:T(8,128)(2,1)S(1)}, bf16[256,512]{1,0:T(8,128)(2,1)}, u32[]{:S(2)}) copy-start(bf16[256,512]{1,0:T(8,128)(2,1)} %get-tuple-element.24) | copy-start | bytes 786436
  3.3 5.7 %copy-start.4 = (bf16[256,512]{1,0:T(8,128)(2,1)S(1)}, bf16[256,512]{1,0:T(8,128)(2,1)}, u32[]{:S(2)}) copy-start(bf16[256,512]{1,0:T(8,128)(2,1)} %get-tuple-element.25) | copy-start | bytes 786436
  3.3 7.0 %copy-start.3 = (bf16[256,512]{1,0:T(8,128)(2,1)S(1)}, bf16[256,512]{1,0:T(8,128)(2,1)}, u32[]{:S(2)}) copy-start(bf16[256,512]{1,0:T(8,128)(2,1)} %get-tuple-element.26) | copy-start | bytes 786436
  3.3 7.7 %copy-start.2 = (bf16[256,512]{1,0:T(8,128)(2,1)S(1)}, bf16[256,512]{1,0:T(8,128)(2,1)}, u32[]{:S(2)}) copy-start(bf16[256,512]{1,0:T(8,128)(2,1)} %get-tuple-element.27) | copy-start | bytes 786436
  3.3 17.9 %all-to-all-start = ((bf16[4,256,512]{2,1,0:T(8,128)(2,1)}), bf16[4,256,512]{2,1,0:T(8,128)(2,1)S(1)}, u32[]{:S(2)}, u32[]{:S(2)}) async-start(bf16[4,256,512]{2,1,0:T(8,128)(2,1)} %get-tuple-element.23), calls=%async_computation | async-start | bytes 2097152 | tf_op jit(solution)/shard_map/all_to_all | solution.py:305
  7.7 10.5 %collective-permute-start = (bf16[256,512]{1,0:T(8,128)(2,1)S(1)}, bf16[256,512]{1,0:T(8,128)(2,1)S(1)}, u32[]{:S(2)}, u32[]{:S(2)}) collective-permute-start(bf16[256,512]{1,0:T(8,128)(2,1)S(1)} %copy-done.5), channel_id=1, source_target_pairs={{2,6},{3,7},{4,0},{5,1},{6,10},{7,11},{8,4},{9,5},{10,14},{11,15},... | collective-permute-start | bytes 786440 | tf_op jit(solution)/shard_map/ppermute | solution.py:306
  9.0 12.2 %collective-permute-start.1 = (bf16[256,512]{1,0:T(8,128)(2,1)S(1)}, bf16[256,512]{1,0:T(8,128)(2,1)S(1)}, u32[]{:S(2)}, u32[]{:S(2)}) collective-permute-start(bf16[256,512]{1,0:T(8,128)(2,1)S(1)} %copy-done.4), channel_id=1, source_target_pairs={{2,7},{3,4},{4,1},{5,2},{6,11},{7,8},{8,5},{9,6},{10,15},{11,12},{... | collective-permute-start | bytes 786440 | tf_op jit(solution)/shard_map/ppermute | solution.py:306
  10.4 10.9 %collective-permute-start.2 = (bf16[256,512]{1,0:T(8,128)(2,1)S(1)}, bf16[256,512]{1,0:T(8,128)(2,1)S(1)}, u32[]{:S(2)}, u32[]{:S(2)}) collective-permute-start(bf16[256,512]{1,0:T(8,128)(2,1)S(1)} %copy-done.3), channel_id=1, source_target_pairs={{2,4},{3,5},{4,2},{5,3},{6,8},{7,9},{8,6},{9,7},{10,12},{11,13},{1... | collective-permute-start | bytes 786440 | tf_op jit(solution)/shard_map/ppermute | solution.py:306
  11.0 10.2 %collective-permute-start.3 = (bf16[256,512]{1,0:T(8,128)(2,1)S(1)}, bf16[256,512]{1,0:T(8,128)(2,1)S(1)}, u32[]{:S(2)}, u32[]{:S(2)}) collective-permute-start(bf16[256,512]{1,0:T(8,128)(2,1)S(1)} %copy-done.2), channel_id=1, source_target_pairs={{2,5},{3,6},{4,3},{5,0},{6,9},{7,10},{8,7},{9,4},{10,13},{11,14},{... | collective-permute-start | bytes 786440 | tf_op jit(solution)/shard_map/ppermute | solution.py:306
  11.7 0.7 copy-start.1
  12.5 8.8 %copy-start = (s32[16]{0:T(128)S(1)}, s32[16]{0:T(128)}, u32[]{:S(2)}) copy-start(s32[16]{0:T(128)} %lengths.1) | copy-start | bytes 196
  27.1 48.3 %all-to-all-start.1 = ((bf16[4,256,384]{2,1,0:T(8,128)(2,1)}), bf16[4,256,384]{2,1,0:T(8,128)(2,1)S(1)}, u32[]{:S(2)}, u32[]{:S(2)}) async-start(bf16[4,256,384]{2,1,0:T(8,128)(2,1)} %bitcast.4), calls=%async_computation.1 | async-start | bytes 1572864 | tf_op jit(solution)/shard_map/all_to_all | solution.py:321
  44.0 6.5 %collective-permute-start.5 = (f32[16,128]{1,0:T(8,128)S(1)}, f32[16,128]{1,0:T(8,128)S(1)}, u32[]{:S(2)}, u32[]{:S(2)}) collective-permute-start(f32[16,128]{1,0:T(8,128)S(1)} %get-tuple-element.34), channel_id=1, source_target_pairs={{0,4},{4,0},{8,12},{12,8},{16,20},{20,16},{24,28},{28,24},{1,5},{5... | collective-permute-start | bytes 24584 | tf_op jit(solution)/shard_map/ppermute | solution.py:314
  50.5 5.1 %collective-permute-start.6 = (f32[16,128]{1,0:T(8,128)S(1)}, f32[16,128]{1,0:T(8,128)S(1)}, u32[]{:S(2)}, u32[]{:S(2)}) collective-permute-start(f32[16,128]{1,0:T(8,128)S(1)} %add.13), channel_id=1, source_target_pairs={{0,8},{4,12},{8,0},{12,4},{16,24},{20,28},{24,16},{28,20},{1,9},{5... | collective-permute-start | bytes 24584 | tf_op jit(solution)/shard_map/ppermute | solution.py:315
  53.4 22.1 %collective-permute-start.4 = (bf16[256,384]{1,0:T(8,128)(2,1)S(1)}, bf16[256,384]{1,0:T(8,128)(2,1)S(1)}, u32[]{:S(2)}, u32[]{:S(2)}) collective-permute-start(bf16[256,384]{1,0:T(8,128)(2,1)S(1)} %get-tuple-element.30), channel_id=1, source_target_pairs={{6,2},{7,3},{0,4},{1,5},{10,6},{11,7},{4,8},{5,9},{14,10},{15,11},... | collective-permute-start | bytes 589832 | tf_op jit(solution)/shard_map/ppermute | solution.py:322
  55.6 19.8 %collective-permute-start.7 = (bf16[256,384]{1,0:T(8,128)(2,1)S(1)}, bf16[256,384]{1,0:T(8,128)(2,1)S(1)}, u32[]{:S(2)}, u32[]{:S(2)}) collective-permute-start(bf16[256,384]{1,0:T(8,128)(2,1)S(1)} %get-tuple-element.35), channel_id=1, source_target_pairs={{7,2},{4,3},{1,4},{2,5},{11,6},{8,7},{5,8},{6,9},{15,10},{12,11},{... | collective-permute-start | bytes 589832 | tf_op jit(solution)/shard_map/ppermute | solution.py:322
  59.7 15.7 %collective-permute-start.8 = (bf16[256,384]{1,0:T(8,128)(2,1)S(1)}, bf16[256,384]{1,0:T(8,128)(2,1)S(1)}, u32[]{:S(2)}, u32[]{:S(2)}) collective-permute-start(bf16[256,384]{1,0:T(8,128)(2,1)S(1)} %get-tuple-element.36), channel_id=1, source_target_pairs={{4,2},{5,3},{2,4},{3,5},{8,6},{9,7},{6,8},{7,9},{12,10},{13,11},{1... | collective-permute-start | bytes 589832 | tf_op jit(solution)/shard_map/ppermute | solution.py:322
  60.4 15.0 %collective-permute-start.9 = (bf16[256,384]{1,0:T(8,128)(2,1)S(1)}, bf16[256,384]{1,0:T(8,128)(2,1)S(1)}, u32[]{:S(2)}, u32[]{:S(2)}) collective-permute-start(bf16[256,384]{1,0:T(8,128)(2,1)S(1)} %get-tuple-element.37), channel_id=1, source_target_pairs={{5,2},{6,3},{3,4},{0,5},{9,6},{10,7},{7,8},{4,9},{13,10},{14,11},{... | collective-permute-start | bytes 589832 | tf_op jit(solution)/shard_map/ppermute | solution.py:322
  61.1 13.7 %collective-permute-start.10 = (f32[16,128]{1,0:T(8,128)S(1)}, f32[16,128]{1,0:T(8,128)S(1)}, u32[]{:S(2)}, u32[]{:S(2)}) collective-permute-start(f32[16,128]{1,0:T(8,128)S(1)} %add.14), channel_id=1, source_target_pairs={{0,16},{4,20},{8,24},{12,28},{16,0},{20,4},{24,8},{28,12},{1,17},{... | collective-permute-start | bytes 24584 | tf_op jit(solution)/shard_map/ppermute | solution.py:319
